TPU v7x, 32 devices: a whole 2x2x4 slice. The times are simulated.
32 devices in a mesh: cases: 2 (over y), gx: 4 (over z), gy: 2 (over x), gz: 2 (over core).
Axes of the slice: x: 2, y: 2, z: 4, core: 2. Of those that a mesh axis runs over, the one named last changes fastest.
Arguments:
- adjoint_state: float32 [26, 128, 16, 256], P(None, ('cases', 'gx'), 'gy', 'gz'), parts along dimension 1, may hold values from -6 to 6
- macroscopic_state: float32 [5, 128, 16, 256], P(None, ('cases', 'gx'), 'gy', 'gz'), parts along dimension 1, may hold values from -0.3 to 2, as said below
- design: float32 [128, 16, 256], P(('cases', 'gx'), 'gy', 'gz'), parts along dimension 0, may hold values from 0.05 to 1
- solid: int32 [128, 16, 256], P(('cases', 'gx'), 'gy', 'gz'), parts along dimension 0, may hold values 0 or 1
- heated: int32 [128, 16], P(('cases', 'gx'), 'gy'), parts along dimension 0, may hold values 0 or 1
- face_labels: int32 [4, 16, 256], P('cases', 'gy', 'gz'), parts along dimension 0, may hold values from 0 to 1
- radius: int32 [128], P('cases'), parts along dimension 0, may hold values from 1 to 2, as said below
Outputs:
- adjoint_next: float32 [26, 128, 16, 256], P(None, ('cases', 'gx'), 'gy', 'gz'), parts along dimension 1
- sensitivity: float32 [128, 16, 256], P(('cases', 'gx'), 'gy', 'gz'), parts along dimension 0
There are 2 independent parts, one for each index of `cases`. A program takes and returns all parts, laid end to end along the dimension named above; each array names one. Nothing has to cross between parts.
Inputs may be any that keep to these rules, and one draw needn't show every extreme that they name: `macroscopic_state`: component 0 is a positive density, 1 to 3 a velocity, 4 a temperature. `face_labels`: 0 is a closed wall cell of the face, 1 an open one. `radius`: both radii 1 and 2 occur.
All inputs are finite; a program needn't handle non-finite values. No bound on the sum of `solid` or of `heated` on one device may be relied on, other than what follows from the above.
Results may differ from a plain program's by a relative error of at most 0.000088.
Values sent between devices are 32-bit elements; how exact they have to be, the bound alone decides.
A program may use at most 64 MiB of HBM per device.

v0:
```python
import jax
import jax.numpy as jnp
from jax import lax
from jax.experimental import pallas as pl
from jax.experimental.pallas import tpu as pltpu
from jax.sharding import PartitionSpec as P

VECTORS = [
    (0, 0, 0),
    (1, 0, 0), (-1, 0, 0), (0, 1, 0), (0, -1, 0), (0, 0, 1), (0, 0, -1),
    (1, 1, 0), (-1, -1, 0), (1, -1, 0), (-1, 1, 0),
    (1, 0, 1), (-1, 0, -1), (1, 0, -1), (-1, 0, 1),
    (0, 1, 1), (0, -1, -1), (0, 1, -1), (0, -1, 1),
]
VECTORS = VECTORS + VECTORS[:7]
OPP = [0, 2, 1, 4, 3, 6, 5, 8, 7, 10, 9, 12, 11, 14, 13, 16, 15, 18, 17, 19, 21, 20, 23, 22, 25, 24]
X_FROM = ([2, 8, 10, 12, 14, 21], [1, 7, 9, 11, 13, 20])
Y_FROM = ([4, 8, 9, 16, 18, 23], [3, 7, 10, 15, 17, 22])
Z_PAIRS = [(5, 6, 0), (15, 17, 16), (18, 16, 32), (24, 25, 48), (11, 13, 64), (14, 12, 96)]
Z_BASE = {i: base for a, b, base in Z_PAIRS for i in (a, b)}
MESH = pl.DeviceIdType.MESH
W0, W1, W2 = 1.0 / 3.0, 1.0 / 18.0, 1.0 / 36.0

ROUND_1 = (
    [(dx, 0, 0) for dx in (1, -1)]
    + [(0, dy, 0) for dy in (1, -1)]
    + [(0, 0, 1)]
    + [(dx, dy, 0) for dx in (1, -1) for dy in (1, -1)]
    + [(dx, 0, 1) for dx in (1, -1)]
    + [(0, dy, 1) for dy in (1, -1)]
)
ROUND_2 = ROUND_1 + [(dx, dy, 1) for dx in (1, -1) for dy in (1, -1)]


def kernel(
    nx, state, macro, design, solid, heated, faces, radius, out, sens,
    S, MA, DE, SO, HE, FA, O, G, xs, xr, ys, yh, zs, zh, xzr, yzr,
    tp, tys, trow, tyz, tzs, tz, zr, Wb, hT, SE,
    in_sem, out_sem, send1, recv1, send2, recv2,
):
    f32 = jnp.float32
    px, py = lax.axis_size("gx"), lax.axis_size("gy")
    me_c, me_x = lax.axis_index("cases"), lax.axis_index("gx")
    me_y, me_z = lax.axis_index("gy"), lax.axis_index("gz")

    def has(d):
        flag = None
        for delta, me, count in ((d[0], me_x, px), (d[1], me_y, py)):
            if delta == 0:
                continue
            here = me < count - 1 if delta > 0 else me > 0
            flag = here if flag is None else jnp.logical_and(flag, here)
        return flag

    def when(flag, body):
        if flag is None:
            body()
        else:
            pl.when(flag)(body)

    def target(d):
        return (me_c, me_x + d[0], me_y + d[1], 1 - me_z if d[2] else me_z)

    loads = [
        pltpu.make_async_copy(state, S.at[:, 1 : 1 + nx], in_sem.at[0]),
        pltpu.make_async_copy(macro, MA, in_sem.at[1]),
        pltpu.make_async_copy(design, DE, in_sem.at[2]),
        pltpu.make_async_copy(solid, SO, in_sem.at[3]),
        pltpu.make_async_copy(heated, HE, in_sem.at[4]),
        pltpu.make_async_copy(faces, FA, in_sem.at[5]),
    ]
    for load in loads:
        load.start()

    trow[...] = jnp.zeros_like(trow)
    tyz[...] = jnp.zeros_like(tyz)
    tz[...] = jnp.zeros_like(tz)
    tp[0:2] = jnp.zeros((2, 8, 128), f32)
    tp[nx + 2 : nx + 4] = jnp.zeros((2, 8, 128), f32)

    barrier = pltpu.get_barrier_semaphore()
    for d in ROUND_2:
        def greet(d=d):
            pl.semaphore_signal(barrier, inc=1, device_id=target(d), device_id_type=MESH)
        when(has(d), greet)

    lane = lax.broadcasted_iota(jnp.int32, (8, 128), 1)
    sub = lax.broadcasted_iota(jnp.int32, (8, 128), 0)
    edge = 127 * me_z
    mine = 127 - edge

    for load in loads:
        load.wait()

    for side, (x_at, y_at) in enumerate(((nx, 7), (1, 0))):
        for j in range(6):
            xs[side, j] = S[X_FROM[side][j], x_at]
            ys[side, j] = S[Y_FROM[side][j], 1 : 1 + nx, y_at, :]

    def pack(x, acc):
        for first, second, base in Z_PAIRS:
            v = S[jnp.where(me_z == 1, first, second), x + 1]
            moved = pltpu.roll(v, lax.rem(base + x - mine + 256, 128), 1)
            acc = jnp.where(lane == base + x, moved, acc)
        return acc

    zs[...] = lax.fori_loop(0, nx, pack, jnp.zeros((8, 128), f32), unroll=True)

    beside_x = jnp.where(me_x > 0, 1, 0) + jnp.where(me_x < px - 1, 1, 0)
    beside_y = jnp.where(me_y > 0, 1, 0) + jnp.where(me_y < py - 1, 1, 0)
    pl.semaphore_wait(barrier, 2 * (beside_x + 1) * (beside_y + 1) - 1)

    def refs_1(d):
        dx, dy, dz = d
        side_x, side_y = (0 if dx > 0 else 1), (0 if dy > 0 else 1)
        if dx and dy:
            j = next(k for k, i in enumerate(Y_FROM[side_y]) if VECTORS[i][0] == -dx)
            if dx > 0:
                return ys.at[side_y, j, nx - 8 : nx], yh.at[side_y, j, 0:8]
            return ys.at[side_y, j, 0:8], yh.at[side_y, j, nx + 8 : nx + 16]
        if dx and dz:
            pair = (14, 12) if dx > 0 else (11, 13)
            return S.at[jnp.where(me_z == 1, pair[0], pair[1]), nx if dx > 0 else 1], xzr.at[side_x]
        if dy and dz:
            j = jnp.where(me_z == 1, 4, 3) if dy > 0 else jnp.where(me_z == 1, 3, 4)
            return ys.at[side_y, j], yzr.at[side_y]
        if dx:
            return xs.at[side_x], xr.at[side_x]
        if dy:
            return ys.at[side_y], yh.at[side_y, :, 8 : 8 + nx]
        return zs, zh

    def refs_2(d):
        dx, dy, dz = d
        side_y = 0 if dy > 0 else 1
        if dy:
            into = tyz if dz else trow
            if dx > 0:
                return tys.at[side_y, :, nx - 8 : nx], into.at[side_y, :, 0:8]
            if dx < 0:
                return tys.at[side_y, :, 0:8], into.at[side_y, :, nx + 8 : nx + 16]
            return tys.at[side_y], into.at[side_y, :, 8 : 8 + nx]
        if dz:
            return tzs, tz.at[0 if dx == 0 else 1 if dx > 0 else 2]
        if dx > 0:
            return tp.at[nx : nx + 2], tp.at[0:2]
        return tp.at[2:4], tp.at[nx + 2 : nx + 4]

    def copies(messages, refs, sends, recvs):
        made = []
        for n, d in enumerate(messages):
            src, dst = refs(d)
            made.append(
                pltpu.make_async_remote_copy(
                    src_ref=src, dst_ref=dst, send_sem=sends.at[n], recv_sem=recvs.at[n],
                    device_id=target(d), device_id_type=MESH,
                )
            )
        return made

    def start(messages, made):
        for d, copy in zip(messages, made):
            when(has(d), copy.start)

    def arrive(messages, made):
        for d, copy in zip(messages, made):
            when(has((-d[0], -d[1], d[2])), copy.wait_recv)

    def leave(messages, made):
        for d, copy in zip(messages, made):
            when(has(d), copy.wait_send)

    round_1 = copies(ROUND_1, refs_1, send1, recv1)
    start(ROUND_1, round_1)

    hT[...] = jnp.zeros_like(hT)
    hT[:, 0:nx] = jnp.where(HE[...] == 1, 1.0, 0.0)

    core = jnp.full((8, 128), me_z, jnp.int32)
    col_p = (lane == 0) & (core == 0)
    col_m = (lane == 127) & (core == 1)
    out_z = {1: (lane == 127) & (core == 1), -1: (lane == 0) & (core == 0)}
    at_y = jnp.full((8, 128), me_y, jnp.int32)
    out_y = {1: (sub == 7) & (at_y == py - 1), -1: (sub == 0) & (at_y == 0)}
    face = {1: FA[1] == 1, -1: FA[0] == 1}
    heat_lane = (lane == 0) & (core == 0)

    arrive(ROUND_1, round_1)

    for side, at in ((0, 0), (1, nx + 1)):
        for j in range(6):
            S[X_FROM[side][j], at] = xr[side, j]
    lane_r = lax.broadcasted_iota(jnp.int32, (nx, 128), 1)
    core_r = jnp.full((nx, 128), me_z, jnp.int32)
    for side in (0, 1):
        for j in (3, 4):
            up = VECTORS[Y_FROM[side][j]][2] > 0
            mask = (lane_r == (0 if up else 127)) & (core_r == (0 if up else 1))
            yh[side, j, 8 : 8 + nx] = jnp.where(mask, yzr[side], yh[side, j, 8 : 8 + nx])
    cols = zh[...]
    cols = jnp.where(lane == 80, pltpu.roll(xzr[1], lax.rem(80 - edge + 128, 128), 1), cols)
    cols = jnp.where(lane == 95, pltpu.roll(xzr[0], lax.rem(95 - edge + 128, 128), 1), cols)
    zh[...] = cols

    first_slab = me_x * nx

    def slab_a(x, carry):
        cols = zh[...]
        at_x = jnp.full((8, 128), first_slab + x, jnp.int32)
        out_x = {1: at_x == px * nx - 1, -1: at_x == 0}
        column = {}
        for first, second, base in Z_PAIRS:
            k = base + x + VECTORS[first][0]
            column[base] = pltpu.roll(cols, lax.rem(edge - k + 256, 128), 1)
        g = []
        for i in range(26):
            cx, cy, cz = VECTORS[i]
            v = S[i, x + 1 + cx]
            if cz:
                v = jnp.where(col_p if cz > 0 else col_m, column[Z_BASE[i]], v)
            if cy:
                side = 0 if cy < 0 else 1
                row = yh[side, Y_FROM[side].index(i), pl.ds(8 + x + cx, 1), :]
                v = jnp.where(sub == (0 if cy > 0 else 7), row, v)
                v = pltpu.roll(v, 7 if cy > 0 else 1, 0)
            if cz:
                v = pltpu.roll(v, 127 if cz > 0 else 1, 1)
            if (cx, cy, cz) != (0, 0, 0):
                bounce = S[OPP[i], x + 1]
                leaves = None
                if cy:
                    leaves = out_y[cy]
                if cz:
                    leaves = out_z[cz] if leaves is None else leaves | out_z[cz]
                if cx:
                    opened = out_x[cx] & face[cx]
                    if leaves is not None:
                        opened = opened & jnp.logical_not(leaves)
                    bounce = jnp.where(opened, 0.0, bounce)
                    leaves = out_x[cx] if leaves is None else leaves | out_x[cx]
                v = jnp.where(leaves, bounce, v)
            O[i, x] = v
            g.append(v)
        s = {i: g[i] + g[i + 1] for i in range(1, 19, 2)}
        d = {i: g[i] - g[i + 1] for i in range(1, 19, 2)}
        xy, xz, yz = s[7] + s[9], s[11] + s[13], s[15] + s[17]
        g0 = W0 * g[0] + W1 * (s[1] + s[3] + s[5]) + W2 * (xy + xz + yz)
        g1x = W1 * d[1] + W2 * ((d[7] + d[9]) + (d[11] + d[13]))
        g1y = W1 * d[3] + W2 * ((d[7] - d[9]) + (d[15] + d[17]))
        g1z = W1 * d[5] + W2 * ((d[11] - d[13]) + (d[15] - d[17]))
        gxx = W1 * s[1] + W2 * (xy + xz)
        gyy = W1 * s[3] + W2 * (xy + yz)
        gzz = W1 * s[5] + W2 * (xz + yz)
        gxy, gxz, gyz = W2 * (s[7] - s[9]), W2 * (s[11] - s[13]), W2 * (s[15] - s[17])
        q0 = 0.25 * g[19] + 0.125 * ((g[20] + g[21]) + (g[22] + g[23]) + (g[24] + g[25]))
        q1x, q1y, q1z = (0.125 * (g[i] - g[i + 1]) for i in (20, 22, 24))
        rho, ux, uy, uz, temp = (MA[k, x] for k in range(5))
        fluid = jnp.where(SO[x] == 1, 0.0, 1.0)
        a = DE[x] * fluid
        aa = a * a
        tx = gxx * ux + gxy * uy + gxz * uz
        ty = gxy * ux + gyy * uy + gyz * uz
        tzz = gxz * ux + gyz * uy + gzz * uz
        quad = ux * tx + uy * ty + uz * tzz
        speed = ux * ux + uy * uy + uz * uz
        first_u = g1x * ux + g1y * uy + g1z * uz
        adv = q1x * ux + q1y * uy + q1z * uz
        both = 9.0 * quad - 3.0 * speed * g0
        buoy = 5.0 * a * temp / rho
        G[0, x] = 1.6 * (g0 - aa * (0.5 * both)) - buoy * adv
        G[1, x] = 1.6 * (3.0 * a * g1x + aa * (9.0 * tx - 3.0 * g0 * ux)) + buoy * q1x
        G[2, x] = 1.6 * (3.0 * a * g1y + aa * (9.0 * ty - 3.0 * g0 * uy)) + buoy * q1y
        G[3, x] = 1.6 * (3.0 * a * g1z + aa * (9.0 * tzz - 3.0 * g0 * uz)) + buoy * q1z
        hot = jnp.where(heat_lane, pltpu.roll(hT[...], lax.rem(128 - x, 128), 1), 0.0)
        G[4, x] = 1.25 * (q0 + 4.0 * a * adv) + 0.5 * hot
        term = fluid * (1.6 * rho * (3.0 * first_u + a * both) + 5.0 * temp * adv)
        reach = jnp.full((8, 128), radius[first_slab + x], jnp.int32)
        tp[x + 2] = term * jnp.where(reach == 2, 1.0 / 125.0, 1.0 / 27.0)
        return carry

    lax.fori_loop(0, nx, slab_a, 0)

    for r in (0, 1):
        tys[0, r] = tp[2 : 2 + nx, 6 + r, :]
        tys[1, r] = tp[2 : 2 + nx, r, :]
    from_lane = 126 * (1 - me_z)
    packed = jnp.zeros((8, 128), f32)
    for x in range(nx):
        moved = pltpu.roll(tp[x + 2], lax.rem(2 * x + 4 - from_lane + 128, 128), 1)
        packed = jnp.where((lane >= 2 * x + 4) & (lane < 2 * x + 6), moved, packed)
    tzs[...] = packed

    round_2 = copies(ROUND_2, refs_2, send2, recv2)
    start(ROUND_2, round_2)

    def slab_b(x, carry):
        walls = SO[x] == 1
        p, mx, my, mz, h = (G[k, x] for k in range(5))
        g = [O[i, x] for i in range(26)]
        O[0, x] = jnp.where(walls, g[0], -0.6 * g[0] + p)
        for i in range(1, 19, 2):
            cx, cy, cz = VECTORS[i]
            along = None
            for c, m in ((cx, mx), (cy, my), (cz, mz)):
                if c:
                    along = m if along is None else along + m if c > 0 else along - m
            O[i, x] = jnp.where(walls, g[i + 1], -0.6 * g[i] + (p + along))
            O[i + 1, x] = jnp.where(walls, g[i], -0.6 * g[i + 1] + (p - along))
        for i in range(19, 26):
            O[i, x] = -0.25 * g[i] + h
        return carry

    stores = []
    for n in range(4):
        lax.fori_loop(n * (nx // 4), (n + 1) * (nx // 4), slab_b, 0)
        part = pl.ds(n * (nx // 4), nx // 4)
        stores.append(pltpu.make_async_copy(O.at[:, part], out.at[:, part], out_sem.at[n]))
        stores[-1].start()

    arrive(ROUND_2, round_2)

    def along_z(v, enter, lanes, at_core):
        enter_p = jnp.where(at_core == 0, enter, 0.0)
        enter_m = jnp.where(at_core == 1, enter, 0.0)
        one = v + pltpu.roll(jnp.where(lanes == 0, enter_p, v), 127, 1)
        one = one + pltpu.roll(jnp.where(lanes == 127, enter_m, v), 1, 1)
        two = one + pltpu.roll(jnp.where(lanes < 2, enter_p, v), 126, 1)
        two = two + pltpu.roll(jnp.where(lanes >= 126, enter_m, v), 2, 1)
        return one, two

    lane_t = lax.broadcasted_iota(jnp.int32, (nx + 16, 128), 1)
    core_t = jnp.full((nx + 16, 128), me_z, jnp.int32)
    for side in (0, 1):
        for r in (0, 1):
            one, two = along_z(trow[side, r], tyz[side, r], lane_t, core_t)
            zr[0, side, r] = one
            zr[1, side, r] = two

    low = pltpu.roll(tz[1], 128 - 2 * nx, 1)
    high = pltpu.roll(tz[2], 2 * nx, 1)
    columns = jnp.where(lane < 4, low, jnp.where(lane >= 2 * nx + 4, high, tz[0]))
    tz[0] = columns

    def slab_c(n, carry):
        at = jnp.clip(first_slab + n - 2, 0, px * nx - 1)
        wide = jnp.full((8, 128), radius[at], jnp.int32) == 2
        enter = pltpu.roll(tz[0], lax.rem(126 * me_z - 2 * n + 256, 128), 1)
        one, two = along_z(tp[n], enter, lane, core)
        v = jnp.where(wide, two, one)
        here = pl.ds(6 + n, 1)
        up_1 = jnp.where(wide, zr[1, 1, 0, here, :], zr[0, 1, 0, here, :])
        up_2 = zr[1, 1, 1, here, :]
        down_1 = jnp.where(wide, zr[1, 0, 1, here, :], zr[0, 0, 1, here, :])
        down_2 = zr[1, 0, 0, here, :]
        v_up = jnp.where(sub == 0, up_1, v)
        v_down = jnp.where(sub == 7, down_1, v)
        one = v + pltpu.roll(v_up, 7, 0) + pltpu.roll(v_down, 1, 0)
        two = one + pltpu.roll(jnp.where(sub == 1, up_2, v_up), 6, 0)
        two = two + pltpu.roll(jnp.where(sub == 6, down_2, v_down), 2, 0)
        Wb[0, n] = jnp.where(wide, two, one)
        Wb[1, n] = jnp.where(wide, two, 0.0)
        return carry

    lax.fori_loop(0, nx + 4, slab_c, 0, unroll=4)
    for x in range(nx):
        SE[x] = (Wb[0, x + 1] + Wb[0, x + 2]) + (Wb[0, x + 3] + (Wb[1, x] + Wb[1, x + 4]))
    last = pltpu.make_async_copy(SE, sens, out_sem.at[4])
    last.start()
    leave(ROUND_1, round_1)
    leave(ROUND_2, round_2)
    for store in stores:
        store.wait()
    last.wait()


def body(adjoint_state, macroscopic_state, design, solid, heated, face_labels, radius):
    count, nx, ny, nz = adjoint_state.shape
    assert (count, ny, nz) == (26, 8, 128) and lax.axis_size("gz") == 2 and nx == 16
    f32 = jnp.float32
    any_space = pl.BlockSpec(memory_space=pl.ANY)
    vmem = lambda *shape: pltpu.VMEM(shape, f32)
    dma = lambda n: pltpu.SemaphoreType.DMA((n,))

    def run(*refs):
        kernel(nx, *refs)

    return pl.pallas_call(
        run,
        out_shape=(
            jax.ShapeDtypeStruct(adjoint_state.shape, f32),
            jax.ShapeDtypeStruct(design.shape, f32),
        ),
        in_specs=[any_space] * 6 + [pl.BlockSpec(memory_space=pltpu.SMEM)],
        out_specs=(any_space, any_space),
        scratch_shapes=[
            vmem(26, nx + 2, 8, 128),
            vmem(5, nx, 8, 128),
            vmem(nx, 8, 128),
            pltpu.VMEM((nx, 8, 128), jnp.int32),
            pltpu.VMEM((8, nx), jnp.int32),
            pltpu.VMEM((2, 8, 128), jnp.int32),
            vmem(26, nx, 8, 128),
            vmem(5, nx, 8, 128),
            vmem(2, 6, 8, 128),
            vmem(2, 6, 8, 128),
            vmem(2, 6, nx, 128),
            vmem(2, 6, nx + 16, 128),
            vmem(8, 128),
            vmem(8, 128),
            vmem(2, 8, 128),
            vmem(2, nx, 128),
            vmem(nx + 4, 8, 128),
            vmem(2, 2, nx, 128),
            vmem(2, 2, nx + 16, 128),
            vmem(2, 2, nx + 16, 128),
            vmem(8, 128),
            vmem(3, 8, 128),
            vmem(2, 2, 2, nx + 16, 128),
            vmem(2, nx + 4, 8, 128),
            vmem(8, 128),
            vmem(nx, 8, 128),
            dma(6), dma(5),
            dma(len(ROUND_1)), dma(len(ROUND_1)),
            dma(len(ROUND_2)), dma(len(ROUND_2)),
        ],
        compiler_params=pltpu.CompilerParams(
            collective_id=0, has_side_effects=True, vmem_limit_bytes=24 * 1024 * 1024
        ),
    )(adjoint_state, macroscopic_state, design, solid, heated.T, face_labels, radius)


def solution(mesh):
    placed = (
        P(None, ("cases", "gx"), "gy", "gz"),
        P(None, ("cases", "gx"), "gy", "gz"),
        P(("cases", "gx"), "gy", "gz"),
        P(("cases", "gx"), "gy", "gz"),
        P(("cases", "gx"), "gy"),
        P("cases", "gy", "gz"),
        P("cases"),
    )
    return jax.shard_map(
        body,
        mesh=mesh,
        in_specs=placed,
        out_specs=(P(None, ("cases", "gx"), "gy", "gz"), P(("cases", "gx"), "gy", "gz")),
        check_vma=False,
    )
```

profile of v0, /device:TPU:0, one launch (start us, length us, event | category | flops | bytes accessed | tf_op | source)
XLA Modules:
  0.0 25.9 jit_solution(6268947118888615924)
XLA Ops:
  0.6 0.0 copy-start
  0.6 1.4 %copy-done = f32[26,16,8,128]{3,2,1,0:T(8,128)S(1)} copy-done((f32[26,16,8,128]{3,2,1,0:T(8,128)S(1)}, f32[26,16,8,128]{3,2,1,0:T(8,128)}, u32[]{:S(2)}) %copy-start) | copy-done | bytes 1703960
  2.1 0.0 copy-start.1
  2.1 1.0 %copy-done.1 = f32[5,16,8,128]{3,2,1,0:T(8,128)S(1)} copy-done((f32[5,16,8,128]{3,2,1,0:T(8,128)S(1)}, f32[5,16,8,128]{3,2,1,0:T(8,128)}, u32[]{:S(2)}) %copy-start.1) | copy-done | bytes 327704
  3.1 0.0 copy-start.2
  3.1 0.8 %copy-done.2 = f32[16,8,128]{2,1,0:T(8,128)S(1)} copy-done((f32[16,8,128]{2,1,0:T(8,128)S(1)}, f32[16,8,128]{2,1,0:T(8,128)}, u32[]{:S(2)}) %copy-start.2) | copy-done | bytes 65560
  3.9 0.0 copy-start.3
  3.9 0.8 %copy-done.3 = s32[16,8,128]{2,1,0:T(8,128)S(1)} copy-done((s32[16,8,128]{2,1,0:T(8,128)S(1)}, s32[16,8,128]{2,1,0:T(8,128)}, u32[]{:S(2)}) %copy-start.3) | copy-done | bytes 65560
  4.7 0.0 copy-start.4
  4.7 0.7 %copy-done.4 = s32[2,8,128]{2,1,0:T(8,128)S(1)} copy-done((s32[2,8,128]{2,1,0:T(8,128)S(1)}, s32[2,8,128]{2,1,0:T(8,128)}, u32[]{:S(2)}) %copy-start.4) | copy-done | bytes 8216
  5.4 0.0 copy-start.5
  5.4 0.7 %copy-done.5 = s32[16,8]{0,1:T(8,128)S(1)} copy-done((s32[16,8]{0,1:T(8,128)S(1)}, s32[16,8]{0,1:T(8,128)}, u32[]{:S(2)}) %copy-start.5) | copy-done | bytes 536
  6.1 0.0 copy-start.6
  6.1 0.7 %copy-done.6 = s32[64]{0:T(128)S(1)} copy-done((s32[64]{0:T(128)S(1)}, s32[64]{0:T(128)}, u32[]{:S(2)}) %copy-start.6) | copy-done | bytes 280
  6.8 17.3 %shard_map.86 = (f32[26,16,8,128]{3,2,1,0:T(8,128)S(1)}, f32[16,8,128]{2,1,0:T(8,128)S(1)}) custom-call(f32[26,16,8,128]{3,2,1,0:T(8,128)S(1)} %copy-done, f32[5,16,8,128]{3,2,1,0:T(8,128)S(1)} %copy-done.1, f32[16,8,128]{2,1,0:T(8,128)S(1)} %copy-done.2, s32[16,8,128]{2,1,0:T(8,128)S(1)} %copy-done.3, s32[8,16]{1,0:T(8,128)S(1)} %bitcast.1, ...), custom_call_target="tpu_custom_call" | custom-call | tf_op jit(solution)/shard_map/pallas_call | solution.py:387
  24.1 1.2 %copy.11 = f32[26,16,8,128]{3,2,1,0:T(8,128)} copy(f32[26,16,8,128]{3,2,1,0:T(8,128)S(1)} %get-tuple-element.4) | data formatting | bytes 3407872
  25.2 0.6 %copy.12 = f32[16,8,128]{2,1,0:T(8,128)} copy(f32[16,8,128]{2,1,0:T(8,128)S(1)} %get-tuple-element.5) | data formatting | bytes 131072
Async XLA Ops:
  0.6 1.5 %copy-start = (f32[26,16,8,128]{3,2,1,0:T(8,128)S(1)}, f32[26,16,8,128]{3,2,1,0:T(8,128)}, u32[]{:S(2)}) copy-start(f32[26,16,8,128]{3,2,1,0:T(8,128)} %refs_0_.1) | copy-start | bytes 5111812
  2.1 1.0 %copy-start.1 = (f32[5,16,8,128]{3,2,1,0:T(8,128)S(1)}, f32[5,16,8,128]{3,2,1,0:T(8,128)}, u32[]{:S(2)}) copy-start(f32[5,16,8,128]{3,2,1,0:T(8,128)} %refs_1_.1) | copy-start | bytes 983044
  3.1 0.8 %copy-start.2 = (f32[16,8,128]{2,1,0:T(8,128)S(1)}, f32[16,8,128]{2,1,0:T(8,128)}, u32[]{:S(2)}) copy-start(f32[16,8,128]{2,1,0:T(8,128)} %refs_2_.1) | copy-start | bytes 196612
  3.9 0.8 %copy-start.3 = (s32[16,8,128]{2,1,0:T(8,128)S(1)}, s32[16,8,128]{2,1,0:T(8,128)}, u32[]{:S(2)}) copy-start(s32[16,8,128]{2,1,0:T(8,128)} %refs_3_.1) | copy-start | bytes 196612
  4.7 0.7 %copy-start.4 = (s32[2,8,128]{2,1,0:T(8,128)S(1)}, s32[2,8,128]{2,1,0:T(8,128)}, u32[]{:S(2)}) copy-start(s32[2,8,128]{2,1,0:T(8,128)} %refs_5_.1) | copy-start | bytes 24580
  5.4 0.7 %copy-start.5 = (s32[16,8]{0,1:T(8,128)S(1)}, s32[16,8]{0,1:T(8,128)}, u32[]{:S(2)}) copy-start(s32[16,8]{0,1:T(8,128)} %param.11) | copy-start | bytes 1540
  6.1 0.7 %copy-start.6 = (s32[64]{0:T(128)S(1)}, s32[64]{0:T(128)}, u32[]{:S(2)}) copy-start(s32[64]{0:T(128)} %refs_6_.1) | copy-start | bytes 772
where the time goes:
time: 26.2 us; the launch traced here: 25.9 us
  Pallas kernels  17.3 us (66%)
  local copies, waits for them, and re-layouts  7.95 us (30%)
  between operations  0.66 us (3%)
    pallas_call x1, Pallas kernels, body(): pl.pallas_call(run, out_shape=(jax.ShapeDtypeStruct(adjoint_state.shape,...  17.3 us
    unnamed x16, local copies, waits for them, and re-layouts  7.95 us

commit v1 on v0

--- a/solution.py
+++ b/solution.py
@@ -34,7 +34,7 @@
 
 def kernel(
     nx, state, macro, design, solid, heated, faces, radius, out, sens,
-    S, MA, DE, SO, HE, FA, O, G, xs, xr, ys, yh, zs, zh, xzr, yzr,
+    S, MA, DE, SO, HE, FA, O, xs, xr, ys, yh, zs, zh, xzr, yzr,
     tp, tys, trow, tyz, tzs, tz, zr, Wb, hT, SE,
     in_sem, out_sem, send1, recv1, send2, recv2,
 ):
@@ -267,18 +267,23 @@
         adv = q1x * ux + q1y * uy + q1z * uz
         both = 9.0 * quad - 3.0 * speed * g0
         buoy = 5.0 * a * temp / rho
-        G[0, x] = 1.6 * (g0 - aa * (0.5 * both)) - buoy * adv
-        G[1, x] = 1.6 * (3.0 * a * g1x + aa * (9.0 * tx - 3.0 * g0 * ux)) + buoy * q1x
-        G[2, x] = 1.6 * (3.0 * a * g1y + aa * (9.0 * ty - 3.0 * g0 * uy)) + buoy * q1y
-        G[3, x] = 1.6 * (3.0 * a * g1z + aa * (9.0 * tzz - 3.0 * g0 * uz)) + buoy * q1z
+        O[26, x] = 1.6 * (g0 - aa * (0.5 * both)) - buoy * adv
+        O[27, x] = 1.6 * (3.0 * a * g1x + aa * (9.0 * tx - 3.0 * g0 * ux)) + buoy * q1x
+        O[28, x] = 1.6 * (3.0 * a * g1y + aa * (9.0 * ty - 3.0 * g0 * uy)) + buoy * q1y
+        O[29, x] = 1.6 * (3.0 * a * g1z + aa * (9.0 * tzz - 3.0 * g0 * uz)) + buoy * q1z
         hot = jnp.where(heat_lane, pltpu.roll(hT[...], lax.rem(128 - x, 128), 1), 0.0)
-        G[4, x] = 1.25 * (q0 + 4.0 * a * adv) + 0.5 * hot
+        O[30, x] = 1.25 * (q0 + 4.0 * a * adv) + 0.5 * hot
         term = fluid * (1.6 * rho * (3.0 * first_u + a * both) + 5.0 * temp * adv)
         reach = jnp.full((8, 128), radius[first_slab + x], jnp.int32)
         tp[x + 2] = term * jnp.where(reach == 2, 1.0 / 125.0, 1.0 / 27.0)
         return carry
 
-    lax.fori_loop(0, nx, slab_a, 0)
+    stores = []
+    for n in range(4):
+        lax.fori_loop(n * (nx // 4), (n + 1) * (nx // 4), slab_a, 0, unroll=4)
+        part = pl.ds(n * (nx // 4), nx // 4)
+        stores.append(pltpu.make_async_copy(O.at[:, part], out.at[:, part], out_sem.at[n]))
+        stores[-1].start()
 
     for r in (0, 1):
         tys[0, r] = tp[2 : 2 + nx, 6 + r, :]
@@ -292,30 +297,6 @@
 
     round_2 = copies(ROUND_2, refs_2, send2, recv2)
     start(ROUND_2, round_2)
-
-    def slab_b(x, carry):
-        walls = SO[x] == 1
-        p, mx, my, mz, h = (G[k, x] for k in range(5))
-        g = [O[i, x] for i in range(26)]
-        O[0, x] = jnp.where(walls, g[0], -0.6 * g[0] + p)
-        for i in range(1, 19, 2):
-            cx, cy, cz = VECTORS[i]
-            along = None
-            for c, m in ((cx, mx), (cy, my), (cz, mz)):
-                if c:
-                    along = m if along is None else along + m if c > 0 else along - m
-            O[i, x] = jnp.where(walls, g[i + 1], -0.6 * g[i] + (p + along))
-            O[i + 1, x] = jnp.where(walls, g[i], -0.6 * g[i + 1] + (p - along))
-        for i in range(19, 26):
-            O[i, x] = -0.25 * g[i] + h
-        return carry
-
-    stores = []
-    for n in range(4):
-        lax.fori_loop(n * (nx // 4), (n + 1) * (nx // 4), slab_b, 0)
-        part = pl.ds(n * (nx // 4), nx // 4)
-        stores.append(pltpu.make_async_copy(O.at[:, part], out.at[:, part], out_sem.at[n]))
-        stores[-1].start()
 
     arrive(ROUND_2, round_2)
 
@@ -373,6 +354,25 @@
     last.wait()
 
 
+def finish(pulled, solid, sens_in, out, sens):
+    for x in range(solid.shape[0]):
+        walls = solid[x] == 1
+        p, mx, my, mz, h = (pulled[26 + k, x] for k in range(5))
+        g = [pulled[i, x] for i in range(26)]
+        out[0, x] = jnp.where(walls, g[0], -0.6 * g[0] + p)
+        for i in range(1, 19, 2):
+            cx, cy, cz = VECTORS[i]
+            along = None
+            for c, m in ((cx, mx), (cy, my), (cz, mz)):
+                if c:
+                    along = m if along is None else along + m if c > 0 else along - m
+            out[i, x] = jnp.where(walls, g[i + 1], -0.6 * g[i] + (p + along))
+            out[i + 1, x] = jnp.where(walls, g[i], -0.6 * g[i + 1] + (p - along))
+        for i in range(19, 26):
+            out[i, x] = -0.25 * g[i] + h
+    sens[...] = sens_in[...]
+
+
 def body(adjoint_state, macroscopic_state, design, solid, heated, face_labels, radius):
     count, nx, ny, nz = adjoint_state.shape
     assert (count, ny, nz) == (26, 8, 128) and lax.axis_size("gz") == 2 and nx == 16
@@ -384,10 +384,10 @@
     def run(*refs):
         kernel(nx, *refs)
 
-    return pl.pallas_call(
+    pulled, sens = pl.pallas_call(
         run,
         out_shape=(
-            jax.ShapeDtypeStruct(adjoint_state.shape, f32),
+            jax.ShapeDtypeStruct((31,) + design.shape, f32),
             jax.ShapeDtypeStruct(design.shape, f32),
         ),
         in_specs=[any_space] * 6 + [pl.BlockSpec(memory_space=pltpu.SMEM)],
@@ -399,8 +399,7 @@
             pltpu.VMEM((nx, 8, 128), jnp.int32),
             pltpu.VMEM((8, nx), jnp.int32),
             pltpu.VMEM((2, 8, 128), jnp.int32),
-            vmem(26, nx, 8, 128),
-            vmem(5, nx, 8, 128),
+            vmem(31, nx, 8, 128),
             vmem(2, 6, 8, 128),
             vmem(2, 6, 8, 128),
             vmem(2, 6, nx, 128),
@@ -424,9 +423,23 @@
             dma(len(ROUND_2)), dma(len(ROUND_2)),
         ],
         compiler_params=pltpu.CompilerParams(
-            collective_id=0, has_side_effects=True, vmem_limit_bytes=24 * 1024 * 1024
+            collective_id=0, has_side_effects=True, vmem_limit_bytes=56 * 1024 * 1024
         ),
     )(adjoint_state, macroscopic_state, design, solid, heated.T, face_labels, radius)
+    step = 8
+    cells = pl.BlockSpec((step, 8, 128), lambda n: (n, 0, 0))
+    block = lambda count: pl.BlockSpec((count, step, 8, 128), lambda n: (0, n, 0, 0))
+    return pl.pallas_call(
+        finish,
+        grid=(nx // step,),
+        out_shape=(
+            jax.ShapeDtypeStruct(adjoint_state.shape, f32),
+            jax.ShapeDtypeStruct(design.shape, f32),
+        ),
+        in_specs=[block(31), cells, cells],
+        out_specs=(block(26), cells),
+        compiler_params=pltpu.CompilerParams(vmem_limit_bytes=56 * 1024 * 1024),
+    )(pulled, solid, sens)
 
 
 def solution(mesh):

time: 26.2 us -> 19.1 us (0.73)
  local copies, waits for them, and re-layouts: 7.95 us -> 0 us
  Pallas kernels: 17.3 us -> 18.3 us
    unnamed x16 -> x0, local copies, waits for them, and re-layouts: 7.95 us -> none
    pallas_call x1 -> x2, Pallas kernels: 17.3 us -> 18.3 us  [the longest x1 15.6 us: body(): pl.pallas_call(run, out_shape=(jax.ShapeDtypeStruct((31,) + design.shape,...]
where the time goes in v1:
time: 19.1 us; the launch traced here: 18.9 us
  Pallas kernels  18.3 us (96%)
  between operations  0.64 us (3%)
    pallas_call x1, Pallas kernels, body(): pl.pallas_call(run, out_shape=(jax.ShapeDtypeStruct((31,) + design.shape,...  15.6 us
    pallas_call x1, Pallas kernels, body(): pl.pallas_call(finish, grid=(nx // step,), out_shape=(jax.ShapeDtypeStruc...  2.64 us

profile of v1, /device:TPU:0, one launch (start us, length us, event | category | flops | bytes accessed | tf_op | source)
XLA Modules:
  0.0 18.9 jit_solution(15598537952473661954)
XLA Ops:
  0.6 15.6 %shard_map.86 = (f32[31,16,8,128]{3,2,1,0:T(8,128)}, f32[16,8,128]{2,1,0:T(8,128)}) custom-call(f32[26,16,8,128]{3,2,1,0:T(8,128)} %refs_0_.1, f32[5,16,8,128]{3,2,1,0:T(8,128)} %refs_1_.1, f32[16,8,128]{2,1,0:T(8,128)} %refs_2_.1, s32[16,8,128]{2,1,0:T(8,128)} %solid.1, s32[8,16]{1,0:T(8,128)} %bitcast.1, s32[2,8,128]{2,1,0:T(8,128)} %refs_5_.1, s32[64]{0:T(128)} %refs_6_.1), custom_call_target="tpu_custom_call" | custom-call | tf_op jit(solution)/shard_map/pallas_call | solution.py:387
  16.3 2.6 %shard_map.87 = (f32[26,16,8,128]{3,2,1,0:T(8,128)}, f32[16,8,128]{2,1,0:T(8,128)}) custom-call(f32[31,16,8,128]{3,2,1,0:T(8,128)} %get-tuple-element.4.pulled, s32[16,8,128]{2,1,0:T(8,128)} %solid.1, f32[16,8,128]{2,1,0:T(8,128)} %get-tuple-element.5.sens_in), custom_call_target="tpu_custom_call" | custom-call | tf_op jit(solution)/shard_map/pallas_call | solution.py:432

commit v2 on v1

--- a/solution.py
+++ b/solution.py
@@ -29,7 +29,8 @@
     + [(dx, 0, 1) for dx in (1, -1)]
     + [(0, dy, 1) for dy in (1, -1)]
 )
-ROUND_2 = ROUND_1 + [(dx, dy, 1) for dx in (1, -1) for dy in (1, -1)]
+ROUND_1 = ROUND_1[5:] + ROUND_1[2:4] + ROUND_1[:2] + ROUND_1[4:5]
+ROUND_2 = [(dx, dy, 1) for dx in (1, -1) for dy in (1, -1)] + ROUND_1
 
 
 def kernel(
@@ -342,7 +343,7 @@
         Wb[1, n] = jnp.where(wide, two, 0.0)
         return carry
 
-    lax.fori_loop(0, nx + 4, slab_c, 0, unroll=4)
+    lax.fori_loop(0, nx + 4, slab_c, 0, unroll=10)
     for x in range(nx):
         SE[x] = (Wb[0, x + 1] + Wb[0, x + 2]) + (Wb[0, x + 3] + (Wb[1, x] + Wb[1, x + 4]))
     last = pltpu.make_async_copy(SE, sens, out_sem.at[4])

time: 19.1 us -> 18.4 us (0.963)
  Pallas kernels: 18.3 us -> 17.6 us
    pallas_call x1, Pallas kernels: 15.6 us -> 15 us  [body(): pl.pallas_call(run, out_shape=(jax.ShapeDtypeStruct((31,) + design.shape,...]
where the time goes in v2:
time: 18.4 us; the launch traced here: 18.3 us
  Pallas kernels  17.6 us (96%)
  between operations  0.64 us (3%)
    pallas_call x1, Pallas kernels, body(): pl.pallas_call(run, out_shape=(jax.ShapeDtypeStruct((31,) + design.shape,...  15 us
    pallas_call x1, Pallas kernels, body(): pl.pallas_call(finish, grid=(nx // step,), out_shape=(jax.ShapeDtypeStruc...  2.64 us

profile of v2, /device:TPU:0, one launch (start us, length us, event | category | flops | bytes accessed | tf_op | source)
XLA Modules:
  0.0 18.3 jit_solution(9490157214410699309)
XLA Ops:
  0.6 15.0 %shard_map.86 = (f32[31,16,8,128]{3,2,1,0:T(8,128)}, f32[16,8,128]{2,1,0:T(8,128)}) custom-call(f32[26,16,8,128]{3,2,1,0:T(8,128)} %refs_0_.1, f32[5,16,8,128]{3,2,1,0:T(8,128)} %refs_1_.1, f32[16,8,128]{2,1,0:T(8,128)} %refs_2_.1, s32[16,8,128]{2,1,0:T(8,128)} %solid.1, s32[8,16]{1,0:T(8,128)} %bitcast.1, s32[2,8,128]{2,1,0:T(8,128)} %refs_5_.1, s32[64]{0:T(128)} %refs_6_.1), custom_call_target="tpu_custom_call" | custom-call | tf_op jit(solution)/shard_map/pallas_call | solution.py:388
  15.6 2.6 %shard_map.87 = (f32[26,16,8,128]{3,2,1,0:T(8,128)}, f32[16,8,128]{2,1,0:T(8,128)}) custom-call(f32[31,16,8,128]{3,2,1,0:T(8,128)} %get-tuple-element.4.pulled, s32[16,8,128]{2,1,0:T(8,128)} %solid.1, f32[16,8,128]{2,1,0:T(8,128)} %get-tuple-element.5.sens_in), custom_call_target="tpu_custom_call" | custom-call | tf_op jit(solution)/shard_map/pallas_call | solution.py:433

commit v3 on v2

--- a/solution.py
+++ b/solution.py
@@ -90,8 +90,7 @@
     edge = 127 * me_z
     mine = 127 - edge
 
-    for load in loads:
-        load.wait()
+    loads[0].wait()
 
     for side, (x_at, y_at) in enumerate(((nx, 7), (1, 0))):
         for j in range(6):
@@ -173,6 +172,8 @@
 
     round_1 = copies(ROUND_1, refs_1, send1, recv1)
     start(ROUND_1, round_1)
+    for load in loads[1:]:
+        load.wait()
 
     hT[...] = jnp.zeros_like(hT)
     hT[:, 0:nx] = jnp.where(HE[...] == 1, 1.0, 0.0)
@@ -343,7 +344,7 @@
         Wb[1, n] = jnp.where(wide, two, 0.0)
         return carry
 
-    lax.fori_loop(0, nx + 4, slab_c, 0, unroll=10)
+    lax.fori_loop(0, nx + 4, slab_c, 0, unroll=True)
     for x in range(nx):
         SE[x] = (Wb[0, x + 1] + Wb[0, x + 2]) + (Wb[0, x + 3] + (Wb[1, x] + Wb[1, x + 4]))
     last = pltpu.make_async_copy(SE, sens, out_sem.at[4])

time: 18.4 us -> 18.2 us (0.989)
  Pallas kernels: 17.6 us -> 17.4 us
    pallas_call x1, Pallas kernels: 15 us -> 14.8 us  [body(): pl.pallas_call(run, out_shape=(jax.ShapeDtypeStruct((31,) + design.shape,...]
where the time goes in v3:
time: 18.2 us; the launch traced here: 18.1 us
  Pallas kernels  17.4 us (96%)
  between operations  0.64 us (4%)
    pallas_call x1, Pallas kernels, body(): pl.pallas_call(run, out_shape=(jax.ShapeDtypeStruct((31,) + design.shape,...  14.8 us
    pallas_call x1, Pallas kernels, body(): pl.pallas_call(finish, grid=(nx // step,), out_shape=(jax.ShapeDtypeStruc...  2.64 us

profile of v3, /device:TPU:0, one launch (start us, length us, event | category | flops | bytes accessed | tf_op | source)
XLA Modules:
  0.0 18.1 jit_solution(13689524511198454138)
XLA Ops:
  0.6 14.8 %shard_map.86 = (f32[31,16,8,128]{3,2,1,0:T(8,128)}, f32[16,8,128]{2,1,0:T(8,128)}) custom-call(f32[26,16,8,128]{3,2,1,0:T(8,128)} %refs_0_.1, f32[5,16,8,128]{3,2,1,0:T(8,128)} %refs_1_.1, f32[16,8,128]{2,1,0:T(8,128)} %refs_2_.1, s32[16,8,128]{2,1,0:T(8,128)} %solid.1, s32[8,16]{1,0:T(8,128)} %bitcast.1, s32[2,8,128]{2,1,0:T(8,128)} %refs_5_.1, s32[64]{0:T(128)} %refs_6_.1), custom_call_target="tpu_custom_call" | custom-call | tf_op jit(solution)/shard_map/pallas_call | solution.py:389
  15.4 2.6 %shard_map.87 = (f32[26,16,8,128]{3,2,1,0:T(8,128)}, f32[16,8,128]{2,1,0:T(8,128)}) custom-call(f32[31,16,8,128]{3,2,1,0:T(8,128)} %get-tuple-element.4.pulled, s32[16,8,128]{2,1,0:T(8,128)} %solid.1, f32[16,8,128]{2,1,0:T(8,128)} %get-tuple-element.5.sens_in), custom_call_target="tpu_custom_call" | custom-call | tf_op jit(solution)/shard_map/pallas_call | solution.py:434
